TPU v7x, 32 devices: a whole 2x2x4 slice. The times are simulated.
32 devices in a mesh: rows: 4 (over z), segment: 4 (over y, x), tm: 2 (over core).
Axes of the slice: x: 2, y: 2, z: 4, core: 2. Of those that a mesh axis runs over, the one named last changes fastest.
Arguments:
- latents: bfloat16 [4, 8, 8, 128, 128], P(None, 'tm', 'rows'), may hold values from -40 to 40
- conv_first: bfloat16 [4, 3, 3, 3, 128, 128], P('segment'), may hold values from -0.109375 to 0.109375
- conv_second: bfloat16 [4, 3, 3, 3, 128, 128], P('segment'), may hold values from -0.109375 to 0.109375
- gain_first: bfloat16 [4, 128], P('segment'), may hold values from 0.099609375 to 1.8984375
- bias_first: bfloat16 [4, 128], P('segment'), may hold values from -1 to 1
- gain_second: bfloat16 [4, 128], P('segment'), may hold values from 0.099609375 to 1.8984375
- bias_second: bfloat16 [4, 128], P('segment'), may hold values from -1 to 1
Outputs:
- decoded: bfloat16 [4, 8, 8, 128, 128], P('segment', 'tm', 'rows')
All inputs are finite; a program needn't handle non-finite values.
Results may differ from a plain program's by a relative error of at most 0.022.
Values may be sent and summed in bfloat16 or wider, within the bound.
A program may use at most 64 MiB of HBM per device.

v0:
```python
import jax
import jax.numpy as jnp
from jax import lax
from jax.sharding import PartitionSpec as P

GROUPS = 32
EPS = 1e-06


def passed_along(value, axis, steps):
    count = lax.axis_size(axis)
    initial, last = (max(0, -steps), min(count, count - steps))
    return lax.ppermute(value, axis, [(source, source + steps) for source in range(initial, last)])


def padded_2(block, sides, width):
    for axis, dim in sides:
        count = lax.axis_size(axis)
        forward = [(i, i + 1) for i in range(count - 1)]
        backward = [(target, source) for source, target in forward]
        low = lax.ppermute(
            lax.slice_in_dim(block, block.shape[dim] - width, None, axis=dim), axis, forward
        )
        high = lax.ppermute(lax.slice_in_dim(block, 0, width, axis=dim), axis, backward)
        block = jnp.concatenate([low, block, high], axis=dim)
    return block


def normalize(values, norm_gain, norm_bias):
    frames, rows_here, columns, channels = values.shape
    width_group = channels // GROUPS
    grouped = values.astype(jnp.float32).reshape(frames, rows_here, columns, GROUPS, width_group)
    totals = lax.psum(
        (jnp.sum(grouped, axis=(0, 1, 2, 4)), jnp.sum(grouped * grouped, axis=(0, 1, 2, 4))), "rows"
    )
    members = frames * rows_here * lax.axis_size("rows") * columns * width_group
    average = totals[0] / members
    squares = totals[1] / members
    inverse = lax.rsqrt(squares - average * average + EPS)
    scaled = (grouped - average[:, None]) * inverse[:, None]
    scaled = scaled.reshape(values.shape) * norm_gain.astype(jnp.float32) + norm_bias.astype(
        jnp.float32
    )
    return jax.nn.silu(scaled).astype(jnp.bfloat16)


def convolve(active, kernel):
    previous = passed_along(active[-2:], "tm", 1)
    extended = jnp.concatenate([previous, active], axis=0)
    padded = padded_2(extended, (("rows", 1),), 1)
    padded = jnp.pad(padded, ((0, 0), (0, 0), (1, 1), (0, 0)))
    result = lax.conv_general_dilated(
        padded[None],
        kernel,
        (1, 1, 1),
        "VALID",
        dimension_numbers=("NDHWC", "DHWIO", "NDHWC"),
        preferred_element_type=jnp.float32,
    )
    return result[0]


def residual_block(values, params):
    first, second, gain_one, bias_one, gain_two, bias_two = params
    active = normalize(values, gain_one, bias_one)
    hidden = convolve(active, first).astype(jnp.bfloat16)
    active = normalize(hidden, gain_two, bias_two)
    return (values.astype(jnp.float32) + convolve(active, second)).astype(jnp.bfloat16)


def body(latents, conv_first, conv_second, gain_first, bias_first, gain_second, bias_second):
    segments = lax.axis_size("segment")
    micro = latents.shape[0]
    per_segment = micro // segments
    position = lax.axis_index("segment")
    small = jnp.stack([gain_first, bias_first, gain_second, bias_second], axis=1)
    small = lax.all_gather(small, "segment", axis=0, tiled=True)
    first = lax.all_gather(conv_first, "segment", axis=0, tiled=True)
    second = lax.all_gather(conv_second, "segment", axis=0, tiled=True)
    outs = []
    for index in range(per_segment):
        values = lax.dynamic_index_in_dim(
            latents, position * per_segment + index, 0, keepdims=False
        )
        for layer in range(first.shape[0]):
            gains = small[layer]
            values = residual_block(
                values, (first[layer], second[layer], gains[0], gains[1], gains[2], gains[3])
            )
        outs.append(values)
    return jnp.stack(outs)


def solution(mesh):
    in_specs = (
        P(None, "tm", "rows", None, None),
        P("segment", None, None, None, None, None),
        P("segment", None, None, None, None, None),
        P("segment", None),
        P("segment", None),
        P("segment", None),
        P("segment", None),
    )
    out_specs = P("segment", "tm", "rows", None, None)
    return jax.shard_map(body, mesh=mesh, in_specs=in_specs, out_specs=out_specs, check_vma=False)
```

profile of v0, /device:TPU:0, one launch (start us, length us, event | category | flops | bytes accessed | tf_op | source)
XLA Modules:
  0.0 296.4 jit_solution(6094731690513591556)
XLA Ops:
  8.6 13.5 %all-reduce.15 = (f32[32]{0:T(128)S(1)}, f32[32]{0:T(128)S(1)}) all-reduce(f32[32]{0:T(128)S(1)} %reduce_sum.195, f32[32]{0:T(128)S(1)} %reduce_sum.189), channel_id=1, replica_groups=mesh['rows'=4,'segment'=4,'tm'=2] {'rows'}, use_global_device_ids=true, to_apply=%region_5.6 | all-reduce | flops 64 | bytes 512 | tf_op jit(solution)/shard_map/psum | solution.py:33
  22.5 8.1 %all_gather.9 = bf16[4,4,128]{2,1,0:T(4,128)(2,1)S(1)} all-gather(bf16[1,4,128]{2,1,0:T(4,128)(2,1)S(1)} %pad_maximum_fusion.8), channel_id=1, replica_groups=mesh['rows'=4,'segment'=4,'tm'=2] {'segment'}, dimensions={0}, use_global_device_ids=true | all-gather | bytes 5120 | tf_op jit(solution)/shard_map/all_gather | solution.py:77
  30.9 1.3 collective-permute-start
  33.2 1.3 collective-permute-start.1
  35.8 3.6 %collective-permute-done.1 = bf16[6,1,128,128]{3,2,1,0:T(8,128)(2,1)S(1)} collective-permute-done((bf16[6,1,128,128]{3,2,1,0:T(8,128)(2,1)S(1)}, bf16[6,1,128,128]{3,2,1,0:T(8,128)(2,1)S(1)}, u32[]{:S(2)}, u32[]{:S(2)}) %collective-permute-start.1) | collective-permute-done | bytes 196640 | tf_op jit(solution)/shard_map/ppermute | solution.py:21
  39.4 4.1 %collective-permute-done.2 = bf16[6,1,128,128]{3,2,1,0:T(8,128)(2,1)S(1)} collective-permute-done((bf16[6,1,128,128]{3,2,1,0:T(8,128)(2,1)S(1)}, bf16[6,1,128,128]{3,2,1,0:T(8,128)(2,1)S(1)}, u32[]{:S(2)}, u32[]{:S(2)}) %collective-permute-start.2) | collective-permute-done | bytes 196640 | tf_op jit(solution)/shard_map/ppermute | solution.py:24
  44.6 14.6 %all-gather.3.cloned.1.call-done = bf16[4,3,3,3,128,128]{5,4,3,2,1,0:T(8,128)(2,1)} async-done(((bf16[1,3,3,3,128,128]{5,4,3,2,1,0:T(8,128)(2,1)}), bf16[4,3,3,3,128,128]{5,4,3,2,1,0:T(8,128)(2,1)}) %all-gather.3.cloned.1.call-update) | async-done | bytes 3538960 | tf_op jit(solution)/shard_map/all_gather | solution.py:78
  59.2 3.3 %fusion.81 = (f32[128]{0:T(128)S(1)}, f32[128]{0:T(128)S(1)}, bf16[4,2,8,17,128]{4,2,3,1,0:T(8,128)(2,1)S(1)}) fusion(pred[8,17]{0,1:T(8,128)(4,1)S(1)} %copy-done.5, bf16[4,3,3,3,128,128]{5,4,3,2,1,0:T(8,128)(2,1)} %all-gather.3.cloned.1.call-done, bf16[6,4,1,7,2,128]{5,3,4,1,0,2:T(8,128)(2,1)S(1)} %slice.249, bf16[6,4,1,8,17,128]{5,3,4,1,0,2:T(8,128)(2,1)S(1)} %copy.62), kind=kOutput, calls=%fused_computation.137 | convolution fusion | flops 966508288 | bytes 2086024 | tf_op jit(solution)/shard_map/conv_general_dilated | solution.py:52
  63.0 11.7 %all-reduce.14 = (f32[32]{0:T(128)S(1)}, f32[32]{0:T(128)S(1)}) all-reduce(f32[32]{0:T(128)S(1)} %reduce_sum.204, f32[32]{0:T(128)S(1)} %reduce_sum.201), channel_id=1, replica_groups=mesh['rows'=4,'segment'=4,'tm'=2] {'rows'}, use_global_device_ids=true, to_apply=%region_11.12 | all-reduce | flops 64 | bytes 512 | tf_op jit(solution)/shard_map/psum | solution.py:33
  78.0 1.3 collective-permute-start.4
  80.6 3.6 %collective-permute-done.4 = bf16[6,1,128,128]{3,2,1,0:T(8,128)(2,1)S(1)} collective-permute-done((bf16[6,1,128,128]{3,2,1,0:T(8,128)(2,1)S(1)}, bf16[6,1,128,128]{3,2,1,0:T(8,128)(2,1)S(1)}, u32[]{:S(2)}, u32[]{:S(2)}) %collective-permute-start.4) | collective-permute-done | bytes 196640 | tf_op jit(solution)/shard_map/ppermute | solution.py:21
  84.3 4.1 %collective-permute-done.5 = bf16[6,1,128,128]{3,2,1,0:T(8,128)(2,1)S(1)} collective-permute-done((bf16[6,1,128,128]{3,2,1,0:T(8,128)(2,1)S(1)}, bf16[6,1,128,128]{3,2,1,0:T(8,128)(2,1)S(1)}, u32[]{:S(2)}, u32[]{:S(2)}) %collective-permute-start.5) | collective-permute-done | bytes 196640 | tf_op jit(solution)/shard_map/ppermute | solution.py:24
  89.4 18.9 %all-gather.5.cloned.1.call-done = bf16[4,3,3,3,128,128]{5,4,3,2,1,0:T(8,128)(2,1)} async-done(((bf16[1,3,3,3,128,128]{5,4,3,2,1,0:T(8,128)(2,1)}), bf16[4,3,3,3,128,128]{5,4,3,2,1,0:T(8,128)(2,1)}) %all-gather.5.cloned.1.call-update) | async-done | bytes 3538960 | tf_op jit(solution)/shard_map/all_gather | solution.py:79
  108.4 3.3 %convolution_select_fusion.6 = f32[4,2,8,17,128]{4,2,3,1,0:T(8,128)S(1)} fusion(bf16[6,4,1,7,2,128]{5,3,4,1,0,2:T(8,128)(2,1)S(1)} %slice.257, bf16[6,4,1,8,17,128]{5,3,4,1,0,2:T(8,128)(2,1)S(1)} %copy.67, bf16[4,3,3,3,128,128]{5,4,3,2,1,0:T(8,128)(2,1)} %all-gather.5.cloned.1.call-done, pred[8,17]{0,1:T(8,128)(4,1)S(1)} %copy-done.5), kind=kOutput, calls=%fused_computation.18 | convolution fusion | flops 965533696 | bytes 2363528 | tf_op jit(solution)/shard_map/conv_general_dilated | solution.py:52
  112.6 11.7 %all-reduce.13 = (f32[32]{0:T(128)S(1)}, f32[32]{0:T(128)S(1)}) all-reduce(f32[32]{0:T(128)S(1)} %reduce_sum.216, f32[32]{0:T(128)S(1)} %reduce_sum.210), channel_id=1, replica_groups=mesh['rows'=4,'segment'=4,'tm'=2] {'rows'}, use_global_device_ids=true, to_apply=%region_17.18 | all-reduce | flops 64 | bytes 512 | tf_op jit(solution)/shard_map/psum | solution.py:33
  124.9 1.3 collective-permute-start.6
  127.3 1.3 collective-permute-start.7
  128.6 1.5 collective-permute-start.8
  130.0 3.5 %collective-permute-done.7 = bf16[6,1,128,128]{3,2,1,0:T(8,128)(2,1)S(1)} collective-permute-done((bf16[6,1,128,128]{3,2,1,0:T(8,128)(2,1)S(1)}, bf16[6,1,128,128]{3,2,1,0:T(8,128)(2,1)S(1)}, u32[]{:S(2)}, u32[]{:S(2)}) %collective-permute-start.7) | collective-permute-done | bytes 196640 | tf_op jit(solution)/shard_map/ppermute | solution.py:21
  133.5 4.1 %collective-permute-done.8 = bf16[6,1,128,128]{3,2,1,0:T(8,128)(2,1)S(1)} collective-permute-done((bf16[6,1,128,128]{3,2,1,0:T(8,128)(2,1)S(1)}, bf16[6,1,128,128]{3,2,1,0:T(8,128)(2,1)S(1)}, u32[]{:S(2)}, u32[]{:S(2)}) %collective-permute-start.8) | collective-permute-done | bytes 196640 | tf_op jit(solution)/shard_map/ppermute | solution.py:24
  138.7 3.3 %fusion.84 = (f32[128]{0:T(128)S(1)}, f32[128]{0:T(128)S(1)}, bf16[4,2,8,17,128]{4,2,3,1,0:T(8,128)(2,1)S(1)}) fusion(pred[8,17]{0,1:T(8,128)(4,1)S(1)} %copy-done.5, bf16[4,3,3,3,128,128]{5,4,3,2,1,0:T(8,128)(2,1)} %all-gather.3.cloned.1.call-done, bf16[6,4,1,7,2,128]{5,3,4,1,0,2:T(8,128)(2,1)S(1)} %slice.265, bf16[6,4,1,8,17,128]{5,3,4,1,0,2:T(8,128)(2,1)S(1)} %copy.72), kind=kOutput, calls=%fused_computation.140 | convolution fusion | flops 966508288 | bytes 2086024 | tf_op jit(solution)/shard_map/conv_general_dilated | solution.py:52
  142.5 8.9 %all-reduce.12 = (f32[32]{0:T(128)S(1)}, f32[32]{0:T(128)S(1)}) all-reduce(f32[32]{0:T(128)S(1)} %reduce_sum.225, f32[32]{0:T(128)S(1)} %reduce_sum.219), channel_id=1, replica_groups=mesh['rows'=4,'segment'=4,'tm'=2] {'rows'}, use_global_device_ids=true, to_apply=%region_23.24 | all-reduce | flops 64 | bytes 512 | tf_op jit(solution)/shard_map/psum | solution.py:33
  152.4 1.3 collective-permute-start.9
  154.7 3.4 %collective-permute-start.10 = (bf16[6,1,128,128]{3,2,1,0:T(8,128)(2,1)S(1)}, bf16[6,1,128,128]{3,2,1,0:T(8,128)(2,1)S(1)}, u32[]{:S(2)}, u32[]{:S(2)}) collective-permute-start(bf16[6,1,128,128]{3,2,1,0:T(8,128)(2,1)S(1)} %get-tuple-element.50), channel_id=1, source_target_pairs={{0,8},{8,16},{16,24},{1,9},{9,17},{17,25},{2,10},{10,18},{18,26},{... | collective-permute-start | bytes 589832 | tf_op jit(solution)/shard_map/ppermute | solution.py:21
  159.4 3.3 %collective-permute-done.10 = bf16[6,1,128,128]{3,2,1,0:T(8,128)(2,1)S(1)} collective-permute-done((bf16[6,1,128,128]{3,2,1,0:T(8,128)(2,1)S(1)}, bf16[6,1,128,128]{3,2,1,0:T(8,128)(2,1)S(1)}, u32[]{:S(2)}, u32[]{:S(2)}) %collective-permute-start.10) | collective-permute-done | bytes 196640 | tf_op jit(solution)/shard_map/ppermute | solution.py:21
  162.7 4.1 %collective-permute-done.11 = bf16[6,1,128,128]{3,2,1,0:T(8,128)(2,1)S(1)} collective-permute-done((bf16[6,1,128,128]{3,2,1,0:T(8,128)(2,1)S(1)}, bf16[6,1,128,128]{3,2,1,0:T(8,128)(2,1)S(1)}, u32[]{:S(2)}, u32[]{:S(2)}) %collective-permute-start.11) | collective-permute-done | bytes 196640 | tf_op jit(solution)/shard_map/ppermute | solution.py:24
  167.9 3.3 %convolution_select_fusion.4 = f32[4,2,8,17,128]{4,2,3,1,0:T(8,128)S(1)} fusion(bf16[6,4,1,7,2,128]{5,3,4,1,0,2:T(8,128)(2,1)S(1)} %slice.273, bf16[6,4,1,8,17,128]{5,3,4,1,0,2:T(8,128)(2,1)S(1)} %copy.77, bf16[4,3,3,3,128,128]{5,4,3,2,1,0:T(8,128)(2,1)} %all-gather.5.cloned.1.call-done, pred[8,17]{0,1:T(8,128)(4,1)S(1)} %copy-done.5), kind=kOutput, calls=%fused_computation.16 | convolution fusion | flops 965533696 | bytes 2363528 | tf_op jit(solution)/shard_map/conv_general_dilated | solution.py:52
  172.1 8.7 %all-reduce.11 = (f32[32]{0:T(128)S(1)}, f32[32]{0:T(128)S(1)}) all-reduce(f32[32]{0:T(128)S(1)} %reduce_sum.234, f32[32]{0:T(128)S(1)} %reduce_sum.231), channel_id=1, replica_groups=mesh['rows'=4,'segment'=4,'tm'=2] {'rows'}, use_global_device_ids=true, to_apply=%region_29.30 | all-reduce | flops 64 | bytes 512 | tf_op jit(solution)/shard_map/psum | solution.py:33
  183.7 3.6 %collective-permute-start.13 = (bf16[6,1,128,128]{3,2,1,0:T(8,128)(2,1)S(1)}, bf16[6,1,128,128]{3,2,1,0:T(8,128)(2,1)S(1)}, u32[]{:S(2)}, u32[]{:S(2)}) collective-permute-start(bf16[6,1,128,128]{3,2,1,0:T(8,128)(2,1)S(1)} %get-tuple-element.48), channel_id=1, source_target_pairs={{0,8},{8,16},{16,24},{1,9},{9,17},{17,25},{2,10},{10,18},{18,26},{... | collective-permute-start | bytes 589832 | tf_op jit(solution)/shard_map/ppermute | solution.py:21
  188.6 3.3 %collective-permute-done.13 = bf16[6,1,128,128]{3,2,1,0:T(8,128)(2,1)S(1)} collective-permute-done((bf16[6,1,128,128]{3,2,1,0:T(8,128)(2,1)S(1)}, bf16[6,1,128,128]{3,2,1,0:T(8,128)(2,1)S(1)}, u32[]{:S(2)}, u32[]{:S(2)}) %collective-permute-start.13) | collective-permute-done | bytes 196640 | tf_op jit(solution)/shard_map/ppermute | solution.py:21
  192.0 4.1 %collective-permute-done.14 = bf16[6,1,128,128]{3,2,1,0:T(8,128)(2,1)S(1)} collective-permute-done((bf16[6,1,128,128]{3,2,1,0:T(8,128)(2,1)S(1)}, bf16[6,1,128,128]{3,2,1,0:T(8,128)(2,1)S(1)}, u32[]{:S(2)}, u32[]{:S(2)}) %collective-permute-start.14) | collective-permute-done | bytes 196640 | tf_op jit(solution)/shard_map/ppermute | solution.py:24
  197.2 3.3 %fusion.87 = (f32[128]{0:T(128)S(1)}, f32[128]{0:T(128)S(1)}, bf16[4,2,8,17,128]{4,2,3,1,0:T(8,128)(2,1)S(1)}) fusion(pred[8,17]{0,1:T(8,128)(4,1)S(1)} %copy-done.5, bf16[4,3,3,3,128,128]{5,4,3,2,1,0:T(8,128)(2,1)} %all-gather.3.cloned.1.call-done, bf16[6,4,1,7,2,128]{5,3,4,1,0,2:T(8,128)(2,1)S(1)} %slice.281, bf16[6,4,1,8,17,128]{5,3,4,1,0,2:T(8,128)(2,1)S(1)} %copy.82), kind=kOutput, calls=%fused_computation.143 | convolution fusion | flops 966508288 | bytes 2086024 | tf_op jit(solution)/shard_map/conv_general_dilated | solution.py:52
  200.9 8.9 %all-reduce.10 = (f32[32]{0:T(128)S(1)}, f32[32]{0:T(128)S(1)}) all-reduce(f32[32]{0:T(128)S(1)} %reduce_sum.291, f32[32]{0:T(128)S(1)} %reduce_sum.288), channel_id=1, replica_groups=mesh['rows'=4,'segment'=4,'tm'=2] {'rows'}, use_global_device_ids=true, to_apply=%region_35.36 | all-reduce | flops 64 | bytes 512 | tf_op jit(solution)/shard_map/psum | solution.py:33
  213.1 3.6 %collective-permute-start.16 = (bf16[6,1,128,128]{3,2,1,0:T(8,128)(2,1)S(1)}, bf16[6,1,128,128]{3,2,1,0:T(8,128)(2,1)S(1)}, u32[]{:S(2)}, u32[]{:S(2)}) collective-permute-start(bf16[6,1,128,128]{3,2,1,0:T(8,128)(2,1)S(1)} %get-tuple-element.46), channel_id=1, source_target_pairs={{0,8},{8,16},{16,24},{1,9},{9,17},{17,25},{2,10},{10,18},{18,26},{... | collective-permute-start | bytes 589832 | tf_op jit(solution)/shard_map/ppermute | solution.py:21
  218.1 3.3 %collective-permute-done.16 = bf16[6,1,128,128]{3,2,1,0:T(8,128)(2,1)S(1)} collective-permute-done((bf16[6,1,128,128]{3,2,1,0:T(8,128)(2,1)S(1)}, bf16[6,1,128,128]{3,2,1,0:T(8,128)(2,1)S(1)}, u32[]{:S(2)}, u32[]{:S(2)}) %collective-permute-start.16) | collective-permute-done | bytes 196640 | tf_op jit(solution)/shard_map/ppermute | solution.py:21
  221.4 4.1 %collective-permute-done.17 = bf16[6,1,128,128]{3,2,1,0:T(8,128)(2,1)S(1)} collective-permute-done((bf16[6,1,128,128]{3,2,1,0:T(8,128)(2,1)S(1)}, bf16[6,1,128,128]{3,2,1,0:T(8,128)(2,1)S(1)}, u32[]{:S(2)}, u32[]{:S(2)}) %collective-permute-start.17) | collective-permute-done | bytes 196640 | tf_op jit(solution)/shard_map/ppermute | solution.py:24
  226.6 3.3 %convolution_select_fusion.2 = f32[4,2,8,17,128]{4,2,3,1,0:T(8,128)S(1)} fusion(bf16[6,4,1,7,2,128]{5,3,4,1,0,2:T(8,128)(2,1)S(1)} %slice.289, bf16[6,4,1,8,17,128]{5,3,4,1,0,2:T(8,128)(2,1)S(1)} %copy.87, bf16[4,3,3,3,128,128]{5,4,3,2,1,0:T(8,128)(2,1)} %all-gather.5.cloned.1.call-done, pred[8,17]{0,1:T(8,128)(4,1)S(1)} %copy-done.5), kind=kOutput, calls=%fused_computation.14 | convolution fusion | flops 965533696 | bytes 2363528 | tf_op jit(solution)/shard_map/conv_general_dilated | solution.py:52
  230.8 8.6 %all-reduce.9 = (f32[32]{0:T(128)S(1)}, f32[32]{0:T(128)S(1)}) all-reduce(f32[32]{0:T(128)S(1)} %reduce_sum.297, f32[32]{0:T(128)S(1)} %reduce_sum.294), channel_id=1, replica_groups=mesh['rows'=4,'segment'=4,'tm'=2] {'rows'}, use_global_device_ids=true, to_apply=%region_41.42 | all-reduce | flops 64 | bytes 512 | tf_op jit(solution)/shard_map/psum | solution.py:33
  242.4 3.6 %collective-permute-start.19 = (bf16[6,1,128,128]{3,2,1,0:T(8,128)(2,1)S(1)}, bf16[6,1,128,128]{3,2,1,0:T(8,128)(2,1)S(1)}, u32[]{:S(2)}, u32[]{:S(2)}) collective-permute-start(bf16[6,1,128,128]{3,2,1,0:T(8,128)(2,1)S(1)} %get-tuple-element.44), channel_id=1, source_target_pairs={{0,8},{8,16},{16,24},{1,9},{9,17},{17,25},{2,10},{10,18},{18,26},{... | collective-permute-start | bytes 589832 | tf_op jit(solution)/shard_map/ppermute | solution.py:21
  247.4 3.3 %collective-permute-done.19 = bf16[6,1,128,128]{3,2,1,0:T(8,128)(2,1)S(1)} collective-permute-done((bf16[6,1,128,128]{3,2,1,0:T(8,128)(2,1)S(1)}, bf16[6,1,128,128]{3,2,1,0:T(8,128)(2,1)S(1)}, u32[]{:S(2)}, u32[]{:S(2)}) %collective-permute-start.19) | collective-permute-done | bytes 196640 | tf_op jit(solution)/shard_map/ppermute | solution.py:21
  250.7 4.1 %collective-permute-done.20 = bf16[6,1,128,128]{3,2,1,0:T(8,128)(2,1)S(1)} collective-permute-done((bf16[6,1,128,128]{3,2,1,0:T(8,128)(2,1)S(1)}, bf16[6,1,128,128]{3,2,1,0:T(8,128)(2,1)S(1)}, u32[]{:S(2)}, u32[]{:S(2)}) %collective-permute-start.20) | collective-permute-done | bytes 196640 | tf_op jit(solution)/shard_map/ppermute | solution.py:24
  255.9 3.3 %fusion.90 = (f32[128]{0:T(128)S(1)}, f32[128]{0:T(128)S(1)}, bf16[4,2,8,17,128]{4,2,3,1,0:T(8,128)(2,1)S(1)}) fusion(pred[8,17]{0,1:T(8,128)(4,1)S(1)} %copy-done.5, bf16[4,3,3,3,128,128]{5,4,3,2,1,0:T(8,128)(2,1)} %all-gather.3.cloned.1.call-done, bf16[6,4,1,7,2,128]{5,3,4,1,0,2:T(8,128)(2,1)S(1)} %slice.297, bf16[6,4,1,8,17,128]{5,3,4,1,0,2:T(8,128)(2,1)S(1)} %copy.92), kind=kOutput, calls=%fused_computation.146 | convolution fusion | flops 966508288 | bytes 2086024 | tf_op jit(solution)/shard_map/conv_general_dilated | solution.py:52
  259.7 8.7 %all-reduce.8 = (f32[32]{0:T(128)S(1)}, f32[32]{0:T(128)S(1)}) all-reduce(f32[32]{0:T(128)S(1)} %reduce_sum.303, f32[32]{0:T(128)S(1)} %reduce_sum.300), channel_id=1, replica_groups=mesh['rows'=4,'segment'=4,'tm'=2] {'rows'}, use_global_device_ids=true, to_apply=%region_47.48 | all-reduce | flops 64 | bytes 512 | tf_op jit(solution)/shard_map/psum | solution.py:33
  271.7 3.6 %collective-permute-start.22 = (bf16[6,1,128,128]{3,2,1,0:T(8,128)(2,1)S(1)}, bf16[6,1,128,128]{3,2,1,0:T(8,128)(2,1)S(1)}, u32[]{:S(2)}, u32[]{:S(2)}) collective-permute-start(bf16[6,1,128,128]{3,2,1,0:T(8,128)(2,1)S(1)} %get-tuple-element.42), channel_id=1, source_target_pairs={{0,8},{8,16},{16,24},{1,9},{9,17},{17,25},{2,10},{10,18},{18,26},{... | collective-permute-start | bytes 589832 | tf_op jit(solution)/shard_map/ppermute | solution.py:21
  275.3 1.6 collective-permute-start.23
  276.8 3.1 %collective-permute-done.22 = bf16[6,1,128,128]{3,2,1,0:T(8,128)(2,1)S(1)} collective-permute-done((bf16[6,1,128,128]{3,2,1,0:T(8,128)(2,1)S(1)}, bf16[6,1,128,128]{3,2,1,0:T(8,128)(2,1)S(1)}, u32[]{:S(2)}, u32[]{:S(2)}) %collective-permute-start.22) | collective-permute-done | bytes 196640 | tf_op jit(solution)/shard_map/ppermute | solution.py:21
  279.9 4.1 %collective-permute-done.23 = bf16[6,1,128,128]{3,2,1,0:T(8,128)(2,1)S(1)} collective-permute-done((bf16[6,1,128,128]{3,2,1,0:T(8,128)(2,1)S(1)}, bf16[6,1,128,128]{3,2,1,0:T(8,128)(2,1)S(1)}, u32[]{:S(2)}, u32[]{:S(2)}) %collective-permute-start.23) | collective-permute-done | bytes 196640 | tf_op jit(solution)/shard_map/ppermute | solution.py:24
  285.1 3.3 %convolution_select_fusion = f32[4,2,8,17,128]{4,2,3,1,0:T(8,128)S(1)} fusion(bf16[6,4,1,7,2,128]{5,3,4,1,0,2:T(8,128)(2,1)S(1)} %slice.305, bf16[6,4,1,8,17,128]{5,3,4,1,0,2:T(8,128)(2,1)S(1)} %copy.97, bf16[4,3,3,3,128,128]{5,4,3,2,1,0:T(8,128)(2,1)} %all-gather.5.cloned.1.call-done, pred[8,17]{0,1:T(8,128)(4,1)S(1)} %copy-done.5), kind=kOutput, calls=%fused_computation.12 | convolution fusion | flops 965533696 | bytes 2363528 | tf_op jit(solution)/shard_map/conv_general_dilated | solution.py:52
  (194 shorter events, 44.3 us)
Async XLA Ops:
  6.5 1.5 copy-start
  6.5 15.9 %copy-start.1 = (bf16[1,128]{1,0:T(2,128)(2,1)S(1)}, bf16[1,128]{1,0:T(2,128)(2,1)}, u32[]{:S(2)}) copy-start(bf16[1,128]{1,0:T(2,128)(2,1)} %param.13) | copy-start | bytes 772
  6.5 16.0 %copy-start.2 = (bf16[1,128]{1,0:T(2,128)(2,1)S(1)}, bf16[1,128]{1,0:T(2,128)(2,1)}, u32[]{:S(2)}) copy-start(bf16[1,128]{1,0:T(2,128)(2,1)} %param.12) | copy-start | bytes 772
  6.5 16.0 %copy-start.3 = (bf16[1,128]{1,0:T(2,128)(2,1)S(1)}, bf16[1,128]{1,0:T(2,128)(2,1)}, u32[]{:S(2)}) copy-start(bf16[1,128]{1,0:T(2,128)(2,1)} %param.11) | copy-start | bytes 772
  6.5 16.0 %copy-start.4 = (bf16[1,128]{1,0:T(2,128)(2,1)S(1)}, bf16[1,128]{1,0:T(2,128)(2,1)}, u32[]{:S(2)}) copy-start(bf16[1,128]{1,0:T(2,128)(2,1)} %param.10) | copy-start | bytes 772
  6.5 52.7 %all-gather.3.cloned.1.call-start = ((), (), s32[]{:S(2)}) async-start(), calls=%async_computation | async-start | bytes 4423680 | tf_op jit(solution)/shard_map/all_gather | solution.py:78
  7.3 101.1 %all-gather.5.cloned.1.call-start = ((), (), s32[]{:S(2)}) async-start(), calls=%async_computation.1 | async-start | bytes 4423680 | tf_op jit(solution)/shard_map/all_gather | solution.py:79
  30.9 2.3 collective-permute-start
  33.2 6.2 %collective-permute-start.1 = (bf16[6,1,128,128]{3,2,1,0:T(8,128)(2,1)S(1)}, bf16[6,1,128,128]{3,2,1,0:T(8,128)(2,1)S(1)}, u32[]{:S(2)}, u32[]{:S(2)}) collective-permute-start(bf16[6,1,128,128]{3,2,1,0:T(8,128)(2,1)S(1)} %get-tuple-element.56), channel_id=1, source_target_pairs={{0,8},{8,16},{16,24},{1,9},{9,17},{17,25},{2,10},{10,18},{18,26},{... | collective-permute-start | bytes 589832 | tf_op jit(solution)/shard_map/ppermute | solution.py:21
  34.5 9.1 %collective-permute-start.2 = (bf16[6,1,128,128]{3,2,1,0:T(8,128)(2,1)S(1)}, bf16[6,1,128,128]{3,2,1,0:T(8,128)(2,1)S(1)}, u32[]{:S(2)}, u32[]{:S(2)}) collective-permute-start(bf16[6,1,128,128]{3,2,1,0:T(8,128)(2,1)S(1)} %get-tuple-element.57), channel_id=1, source_target_pairs={{8,0},{16,8},{24,16},{9,1},{17,9},{25,17},{10,2},{18,10},{26,18},{... | collective-permute-start | bytes 589832 | tf_op jit(solution)/shard_map/ppermute | solution.py:24
  44.1 15.1 %copy-start.5 = (pred[8,17]{0,1:T(8,128)(4,1)S(1)}, pred[8,17]{0,1:T(8,128)(4,1)}, u32[]{:S(2)}) copy-start(pred[8,17]{0,1:T(8,128)(4,1)} %constant.110) | copy-start | bytes 412
  75.7 2.3 collective-permute-start.3
  78.0 6.2 %collective-permute-start.4 = (bf16[6,1,128,128]{3,2,1,0:T(8,128)(2,1)S(1)}, bf16[6,1,128,128]{3,2,1,0:T(8,128)(2,1)S(1)}, u32[]{:S(2)}, u32[]{:S(2)}) collective-permute-start(bf16[6,1,128,128]{3,2,1,0:T(8,128)(2,1)S(1)} %get-tuple-element.54), channel_id=1, source_target_pairs={{0,8},{8,16},{16,24},{1,9},{9,17},{17,25},{2,10},{10,18},{18,26},{... | collective-permute-start | bytes 589832 | tf_op jit(solution)/shard_map/ppermute | solution.py:21
  79.3 9.1 %collective-permute-start.5 = (bf16[6,1,128,128]{3,2,1,0:T(8,128)(2,1)S(1)}, bf16[6,1,128,128]{3,2,1,0:T(8,128)(2,1)S(1)}, u32[]{:S(2)}, u32[]{:S(2)}) collective-permute-start(bf16[6,1,128,128]{3,2,1,0:T(8,128)(2,1)S(1)} %get-tuple-element.55), channel_id=1, source_target_pairs={{8,0},{16,8},{24,16},{9,1},{17,9},{25,17},{10,2},{18,10},{26,18},{... | collective-permute-start | bytes 589832 | tf_op jit(solution)/shard_map/ppermute | solution.py:24
  124.9 2.3 collective-permute-start.6
  127.3 6.2 %collective-permute-start.7 = (bf16[6,1,128,128]{3,2,1,0:T(8,128)(2,1)S(1)}, bf16[6,1,128,128]{3,2,1,0:T(8,128)(2,1)S(1)}, u32[]{:S(2)}, u32[]{:S(2)}) collective-permute-start(bf16[6,1,128,128]{3,2,1,0:T(8,128)(2,1)S(1)} %get-tuple-element.52), channel_id=1, source_target_pairs={{0,8},{8,16},{16,24},{1,9},{9,17},{17,25},{2,10},{10,18},{18,26},{... | collective-permute-start | bytes 589832 | tf_op jit(solution)/shard_map/ppermute | solution.py:21
  128.6 9.1 %collective-permute-start.8 = (bf16[6,1,128,128]{3,2,1,0:T(8,128)(2,1)S(1)}, bf16[6,1,128,128]{3,2,1,0:T(8,128)(2,1)S(1)}, u32[]{:S(2)}, u32[]{:S(2)}) collective-permute-start(bf16[6,1,128,128]{3,2,1,0:T(8,128)(2,1)S(1)} %get-tuple-element.53), channel_id=1, source_target_pairs={{8,0},{16,8},{24,16},{9,1},{17,9},{25,17},{10,2},{18,10},{26,18},{... | collective-permute-start | bytes 589832 | tf_op jit(solution)/shard_map/ppermute | solution.py:24
  152.4 2.3 collective-permute-start.9
  154.7 8.0 %collective-permute-start.10 = (bf16[6,1,128,128]{3,2,1,0:T(8,128)(2,1)S(1)}, bf16[6,1,128,128]{3,2,1,0:T(8,128)(2,1)S(1)}, u32[]{:S(2)}, u32[]{:S(2)}) collective-permute-start(bf16[6,1,128,128]{3,2,1,0:T(8,128)(2,1)S(1)} %get-tuple-element.50), channel_id=1, source_target_pairs={{0,8},{8,16},{16,24},{1,9},{9,17},{17,25},{2,10},{10,18},{18,26},{... | collective-permute-start | bytes 589832 | tf_op jit(solution)/shard_map/ppermute | solution.py:21
  158.1 8.8 %collective-permute-start.11 = (bf16[6,1,128,128]{3,2,1,0:T(8,128)(2,1)S(1)}, bf16[6,1,128,128]{3,2,1,0:T(8,128)(2,1)S(1)}, u32[]{:S(2)}, u32[]{:S(2)}) collective-permute-start(bf16[6,1,128,128]{3,2,1,0:T(8,128)(2,1)S(1)} %get-tuple-element.51), channel_id=1, source_target_pairs={{8,0},{16,8},{24,16},{9,1},{17,9},{25,17},{10,2},{18,10},{26,18},{... | collective-permute-start | bytes 589832 | tf_op jit(solution)/shard_map/ppermute | solution.py:24
  181.4 2.3 collective-permute-start.12
  183.7 8.3 %collective-permute-start.13 = (bf16[6,1,128,128]{3,2,1,0:T(8,128)(2,1)S(1)}, bf16[6,1,128,128]{3,2,1,0:T(8,128)(2,1)S(1)}, u32[]{:S(2)}, u32[]{:S(2)}) collective-permute-start(bf16[6,1,128,128]{3,2,1,0:T(8,128)(2,1)S(1)} %get-tuple-element.48), channel_id=1, source_target_pairs={{0,8},{8,16},{16,24},{1,9},{9,17},{17,25},{2,10},{10,18},{18,26},{... | collective-permute-start | bytes 589832 | tf_op jit(solution)/shard_map/ppermute | solution.py:21
  187.3 8.8 %collective-permute-start.14 = (bf16[6,1,128,128]{3,2,1,0:T(8,128)(2,1)S(1)}, bf16[6,1,128,128]{3,2,1,0:T(8,128)(2,1)S(1)}, u32[]{:S(2)}, u32[]{:S(2)}) collective-permute-start(bf16[6,1,128,128]{3,2,1,0:T(8,128)(2,1)S(1)} %get-tuple-element.49), channel_id=1, source_target_pairs={{8,0},{16,8},{24,16},{9,1},{17,9},{25,17},{10,2},{18,10},{26,18},{... | collective-permute-start | bytes 589832 | tf_op jit(solution)/shard_map/ppermute | solution.py:24
  210.8 2.3 collective-permute-start.15
  213.1 8.3 %collective-permute-start.16 = (bf16[6,1,128,128]{3,2,1,0:T(8,128)(2,1)S(1)}, bf16[6,1,128,128]{3,2,1,0:T(8,128)(2,1)S(1)}, u32[]{:S(2)}, u32[]{:S(2)}) collective-permute-start(bf16[6,1,128,128]{3,2,1,0:T(8,128)(2,1)S(1)} %get-tuple-element.46), channel_id=1, source_target_pairs={{0,8},{8,16},{16,24},{1,9},{9,17},{17,25},{2,10},{10,18},{18,26},{... | collective-permute-start | bytes 589832 | tf_op jit(solution)/shard_map/ppermute | solution.py:21
  216.8 8.8 %collective-permute-start.17 = (bf16[6,1,128,128]{3,2,1,0:T(8,128)(2,1)S(1)}, bf16[6,1,128,128]{3,2,1,0:T(8,128)(2,1)S(1)}, u32[]{:S(2)}, u32[]{:S(2)}) collective-permute-start(bf16[6,1,128,128]{3,2,1,0:T(8,128)(2,1)S(1)} %get-tuple-element.47), channel_id=1, source_target_pairs={{8,0},{16,8},{24,16},{9,1},{17,9},{25,17},{10,2},{18,10},{26,18},{... | collective-permute-start | bytes 589832 | tf_op jit(solution)/shard_map/ppermute | solution.py:24
  240.1 2.3 collective-permute-start.18
  242.4 8.3 %collective-permute-start.19 = (bf16[6,1,128,128]{3,2,1,0:T(8,128)(2,1)S(1)}, bf16[6,1,128,128]{3,2,1,0:T(8,128)(2,1)S(1)}, u32[]{:S(2)}, u32[]{:S(2)}) collective-permute-start(bf16[6,1,128,128]{3,2,1,0:T(8,128)(2,1)S(1)} %get-tuple-element.44), channel_id=1, source_target_pairs={{0,8},{8,16},{16,24},{1,9},{9,17},{17,25},{2,10},{10,18},{18,26},{... | collective-permute-start | bytes 589832 | tf_op jit(solution)/shard_map/ppermute | solution.py:21
  246.1 8.8 %collective-permute-start.20 = (bf16[6,1,128,128]{3,2,1,0:T(8,128)(2,1)S(1)}, bf16[6,1,128,128]{3,2,1,0:T(8,128)(2,1)S(1)}, u32[]{:S(2)}, u32[]{:S(2)}) collective-permute-start(bf16[6,1,128,128]{3,2,1,0:T(8,128)(2,1)S(1)} %get-tuple-element.45), channel_id=1, source_target_pairs={{8,0},{16,8},{24,16},{9,1},{17,9},{25,17},{10,2},{18,10},{26,18},{... | collective-permute-start | bytes 589832 | tf_op jit(solution)/shard_map/ppermute | solution.py:24
  269.4 2.3 collective-permute-start.21
  271.7 8.3 %collective-permute-start.22 = (bf16[6,1,128,128]{3,2,1,0:T(8,128)(2,1)S(1)}, bf16[6,1,128,128]{3,2,1,0:T(8,128)(2,1)S(1)}, u32[]{:S(2)}, u32[]{:S(2)}) collective-permute-start(bf16[6,1,128,128]{3,2,1,0:T(8,128)(2,1)S(1)} %get-tuple-element.42), channel_id=1, source_target_pairs={{0,8},{8,16},{16,24},{1,9},{9,17},{17,25},{2,10},{10,18},{18,26},{... | collective-permute-start | bytes 589832 | tf_op jit(solution)/shard_map/ppermute | solution.py:21
  275.3 8.8 %collective-permute-start.23 = (bf16[6,1,128,128]{3,2,1,0:T(8,128)(2,1)S(1)}, bf16[6,1,128,128]{3,2,1,0:T(8,128)(2,1)S(1)}, u32[]{:S(2)}, u32[]{:S(2)}) collective-permute-start(bf16[6,1,128,128]{3,2,1,0:T(8,128)(2,1)S(1)} %get-tuple-element.43), channel_id=1, source_target_pairs={{8,0},{16,8},{24,16},{9,1},{17,9},{25,17},{10,2},{18,10},{26,18},{... | collective-permute-start | bytes 589832 | tf_op jit(solution)/shard_map/ppermute | solution.py:24
Sparse Core Ops, SparseCore 0:
  9.2 49.9 all-gather.2
  61.1 47.2 all-gather.4
where the time goes:
time: 297 us; the launch traced here: 296 us
  waiting for transfers between devices  103 us (35%)
  blocking collectives  88.7 us (30%)
  starting transfers between devices  43 us (14%)
  matrix products  26.5 us (9%)
  between operations  14.5 us (5%)
  local copies, waits for them, and re-layouts  13.6 us (5%)
  other arithmetic  7.41 us (2%)
    psum x8, blocking collectives, normalize(): lax.psum((jnp.sum(grouped, axis=(0, 1, 2, 4)), jnp.sum(grouped * grouped,...  80.6 us
    ppermute x8, waiting for transfers between devices, padded_2(): lax.ppermute(lax.slice_in_dim(block, 0, width, axis=dim), axis, backward)  33 us
    ppermute x8, waiting for transfers between devices, padded_2(): lax.ppermute(lax.slice_in_dim(block, block.shape[dim] - width, None, axis...  27.2 us
    conv_general_dilated x8, matrix products, convolve(): lax.conv_general_dilated(padded[None], kernel, (1, 1, 1), 'VALID', dimens...  26.5 us
    ppermute x8, starting transfers between devices, padded_2(): lax.ppermute(lax.slice_in_dim(block, block.shape[dim] - width, None, axis...  21.7 us
    all_gather x1, waiting for transfers between devices, body(): second = lax.all_gather(conv_second, 'segment', axis=0, tiled=True)  18.9 us
    all_gather x1, waiting for transfers between devices, body(): first = lax.all_gather(conv_first, 'segment', axis=0, tiled=True)  14.6 us
    ppermute x8, starting transfers between devices, padded_2(): lax.ppermute(lax.slice_in_dim(block, 0, width, axis=dim), axis, backward)  10.8 us
  transfers between devices with their start and end apart: 26, of which 26 were waited for; matrix products, arithmetic and copies ran while one was open for 3% of the time, Pallas kernels for 0%

commit v1 on v0

--- a/solution.py
+++ b/solution.py
@@ -76,7 +76,16 @@
     small = jnp.stack([gain_first, bias_first, gain_second, bias_second], axis=1)
     small = lax.all_gather(small, "segment", axis=0, tiled=True)
     first = lax.all_gather(conv_first, "segment", axis=0, tiled=True)
-    second = lax.all_gather(conv_second, "segment", axis=0, tiled=True)
+    slots = lax.axis_size("segment")
+    spare = sorted(((hop_no, (hop_no + 1) % slots) for hop_no in range(slots)))
+    piece_out = conv_second
+    kept_rows = [piece_out]
+    for u in [*range(1, slots)]:
+        piece_out = lax.ppermute(piece_out, "segment", spare)
+        kept_rows.insert(0, piece_out)
+    e_next = jnp.concatenate(kept_rows, axis=0)
+    b_now = lax.axis_index("segment") + 1
+    second = jnp.roll(e_next, shift=b_now * conv_second.shape[0], axis=0)
     outs = []
     for index in range(per_segment):
         values = lax.dynamic_index_in_dim(

time: 297 us -> 325 us (1.094)
  starting transfers between devices: 43 us -> 55.8 us
  local copies, waits for them, and re-layouts: 13.6 us -> 23.3 us
  blocking collectives: 88.7 us -> 97.6 us
  waiting for transfers between devices: 103 us -> 94.3 us
  other arithmetic: 7.41 us -> 11.3 us
    ppermute x0 -> x3, waiting for transfers between devices: none -> 29.4 us  [body(): piece_out = lax.ppermute(piece_out, 'segment', spare)]
    all_gather x1 -> x0, waiting for transfers between devices: 18.9 us -> none  [body(): second = lax.all_gather(conv_second, 'segment', axis=0, tiled=True)]
    all_gather x1, blocking collectives: 8.08 us -> 23.3 us  [body(): small = lax.all_gather(small, 'segment', axis=0, tiled=True)]
    all_gather x1, waiting for transfers between devices: 14.6 us -> 0.01 us  [body(): first = lax.all_gather(conv_first, 'segment', axis=0, tiled=True)]
    unnamed x20 -> x43, local copies, waits for them, and re-layouts: 2.5 us -> 10.5 us
    ppermute x0 -> x3, starting transfers between devices: none -> 6.83 us  [body(): piece_out = lax.ppermute(piece_out, 'segment', spare)]
    psum x8, blocking collectives: 80.6 us -> 74.3 us  [normalize(): lax.psum((jnp.sum(grouped, axis=(0, 1, 2, 4)), jnp.sum(grouped * grouped,...]
    ppermute x8, starting transfers between devices: 21.7 us -> 27.8 us  [padded_2(): lax.ppermute(lax.slice_in_dim(block, block.shape[dim] - width, None, axis...]
  transfers between devices with their start and end apart: 26 -> 28, of which waited for: 26 -> 24; matrix products, arithmetic and copies ran while one was open for 3% -> 5% of each run, Pallas kernels for 0% -> 0%
where the time goes in v1:
time: 325 us; the launch traced here: 324 us
  blocking collectives  97.6 us (30%)
  waiting for transfers between devices  94.3 us (29%)
  starting transfers between devices  55.8 us (17%)
  matrix products  26.7 us (8%)
  local copies, waits for them, and re-layouts  23.3 us (7%)
  between operations  14.6 us (4%)
  other arithmetic  11.3 us (3%)
    psum x8, blocking collectives, normalize(): lax.psum((jnp.sum(grouped, axis=(0, 1, 2, 4)), jnp.sum(grouped * grouped,...  74.3 us
    ppermute x8, waiting for transfers between devices, padded_2(): lax.ppermute(lax.slice_in_dim(block, 0, width, axis=dim), axis, backward)  32.9 us
    ppermute x3, waiting for transfers between devices, body(): piece_out = lax.ppermute(piece_out, 'segment', spare)  29.4 us
    ppermute x8, starting transfers between devices, padded_2(): lax.ppermute(lax.slice_in_dim(block, block.shape[dim] - width, None, axis...  27.8 us
    conv_general_dilated x8, matrix products, convolve(): lax.conv_general_dilated(padded[None], kernel, (1, 1, 1), 'VALID', dimens...  26.7 us
    ppermute x8, waiting for transfers between devices, padded_2(): lax.ppermute(lax.slice_in_dim(block, block.shape[dim] - width, None, axis...  24.6 us
    all_gather x1, blocking collectives, body(): small = lax.all_gather(small, 'segment', axis=0, tiled=True)  23.3 us
    ppermute x8, starting transfers between devices, padded_2(): lax.ppermute(lax.slice_in_dim(block, 0, width, axis=dim), axis, backward)  10.8 us
  transfers between devices with their start and end apart: 28, of which 24 were waited for; matrix products, arithmetic and copies ran while one was open for 5% of the time, Pallas kernels for 0%

profile of v1, /device:TPU:0, one launch (start us, length us, event | category | flops | bytes accessed | tf_op | source)
XLA Modules:
  0.0 323.7 jit_solution(7942882812171665199)
XLA Ops:
  7.3 3.0 collective-permute-start.6
  10.2 29.4 %collective-permute-done.6 = bf16[1,3,3,3,128,128]{5,4,3,2,1,0:T(8,128)(2,1)S(1)} collective-permute-done((bf16[1,3,3,3,128,128]{5,4,3,2,1,0:T(8,128)(2,1)}, bf16[1,3,3,3,128,128]{5,4,3,2,1,0:T(8,128)(2,1)S(1)}, u32[]{:S(2)}, u32[]{:S(2)}) %collective-permute-start.6) | collective-permute-done | bytes 884768 | tf_op jit(solution)/shard_map/ppermute | solution.py:84
  39.6 1.7 collective-permute-start.7
  42.9 12.0 %all-reduce.15 = (f32[32]{0:T(128)S(1)}, f32[32]{0:T(128)S(1)}) all-reduce(f32[32]{0:T(128)S(1)} %reduce_sum.195, f32[32]{0:T(128)S(1)} %reduce_sum.189), channel_id=1, replica_groups=mesh['rows'=4,'segment'=4,'tm'=2] {'rows'}, use_global_device_ids=true, to_apply=%region_5.6 | all-reduce | flops 64 | bytes 512 | tf_op jit(solution)/shard_map/psum | solution.py:33
  55.6 23.3 %all_gather.6 = bf16[4,4,128]{2,1,0:T(4,128)(2,1)S(1)} all-gather(bf16[1,4,128]{2,1,0:T(4,128)(2,1)S(1)} %pad_maximum_fusion.8), channel_id=1, replica_groups=mesh['rows'=4,'segment'=4,'tm'=2] {'segment'}, dimensions={0}, use_global_device_ids=true | all-gather | bytes 5120 | tf_op jit(solution)/shard_map/all_gather | solution.py:77
  79.5 2.1 collective-permute-start.8
  83.2 1.3 collective-permute-start
  86.2 3.6 %collective-permute-start.1 = (bf16[6,1,128,128]{3,2,1,0:T(8,128)(2,1)}, bf16[6,1,128,128]{3,2,1,0:T(8,128)(2,1)S(1)}, u32[]{:S(2)}, u32[]{:S(2)}) collective-permute-start(bf16[6,1,128,128]{3,2,1,0:T(8,128)(2,1)} %get-tuple-element.56), channel_id=1, source_target_pairs={{0,8},{8,16},{16,24},{1,9},{9,17},{17,25},{2,10},{10,18},{18,26},{... | collective-permute-start | bytes 589832 | tf_op jit(solution)/shard_map/ppermute | solution.py:21
  91.2 3.6 %collective-permute-done.1 = bf16[6,1,128,128]{3,2,1,0:T(8,128)(2,1)S(1)} collective-permute-done((bf16[6,1,128,128]{3,2,1,0:T(8,128)(2,1)}, bf16[6,1,128,128]{3,2,1,0:T(8,128)(2,1)S(1)}, u32[]{:S(2)}, u32[]{:S(2)}) %collective-permute-start.1) | collective-permute-done | bytes 196640 | tf_op jit(solution)/shard_map/ppermute | solution.py:21
  94.8 4.0 %collective-permute-done.2 = bf16[6,1,128,128]{3,2,1,0:T(8,128)(2,1)S(1)} collective-permute-done((bf16[6,1,128,128]{3,2,1,0:T(8,128)(2,1)}, bf16[6,1,128,128]{3,2,1,0:T(8,128)(2,1)S(1)}, u32[]{:S(2)}, u32[]{:S(2)}) %collective-permute-start.2) | collective-permute-done | bytes 196640 | tf_op jit(solution)/shard_map/ppermute | solution.py:24
  105.6 3.6 %fusion.81 = (f32[128]{0:T(128)S(1)}, f32[128]{0:T(128)S(1)}, bf16[4,2,8,17,128]{4,2,3,1,0:T(8,128)(2,1)S(1)}) fusion(pred[8,17]{0,1:T(8,128)(4,1)} %constant.132, bf16[4,3,3,3,128,128]{5,4,3,2,1,0:T(8,128)(2,1)} %all-gather.2.cloned.1.call-done, bf16[6,4,1,7,2,128]{5,3,4,1,0,2:T(8,128)(2,1)} %slice.249, bf16[6,4,1,8,17,128]{5,3,4,1,0,2:T(8,128)(2,1)} %copy-done.2), kind=kOutput, calls=%fused_computation.137 | convolution fusion | flops 966508288 | bytes 2101248 | tf_op jit(solution)/shard_map/conv_general_dilated | solution.py:52
  109.6 10.2 %all-reduce.14 = (f32[32]{0:T(128)S(1)}, f32[32]{0:T(128)S(1)}) all-reduce(f32[32]{0:T(128)S(1)} %reduce_sum.204, f32[32]{0:T(128)S(1)} %reduce_sum.201), channel_id=1, replica_groups=mesh['rows'=4,'segment'=4,'tm'=2] {'rows'}, use_global_device_ids=true, to_apply=%region_11.12 | all-reduce | flops 64 | bytes 512 | tf_op jit(solution)/shard_map/psum | solution.py:33
  123.3 2.4 collective-permute-start.4
  129.0 1.4 collective-permute-done.4
  130.3 4.1 %collective-permute-done.5 = bf16[6,1,128,128]{3,2,1,0:T(8,128)(2,1)S(1)} collective-permute-done((bf16[6,1,128,128]{3,2,1,0:T(8,128)(2,1)S(1)}, bf16[6,1,128,128]{3,2,1,0:T(8,128)(2,1)S(1)}, u32[]{:S(2)}, u32[]{:S(2)}) %collective-permute-start.5) | collective-permute-done | bytes 196640 | tf_op jit(solution)/shard_map/ppermute | solution.py:24
  135.7 3.3 %convolution_select_fusion.6 = f32[4,2,8,17,128]{4,2,3,1,0:T(8,128)S(1)} fusion(bf16[6,4,1,7,2,128]{5,3,4,1,0,2:T(8,128)(2,1)S(1)} %slice.257, bf16[6,4,1,8,17,128]{5,3,4,1,0,2:T(8,128)(2,1)S(1)} %copy.67, bf16[8,3,3,3,128,128]{5,4,3,2,1,0:T(8,128)(2,1)} %constant_dynamic-update-slice_fusion, s32[]{:T(128)S(6)} %select_n.19, pred[8,17]{0,1:T(8,128)(4,1)S(1)} %copy-done.13), kind=kOutput, calls=%fused_computation.18 | convolution fusion | flops 965533696 | bytes 2363532 | tf_op jit(solution)/shard_map/conv_general_dilated | solution.py:52
  140.8 8.7 %all-reduce.13 = (f32[32]{0:T(128)S(1)}, f32[32]{0:T(128)S(1)}) all-reduce(f32[32]{0:T(128)S(1)} %reduce_sum.216, f32[32]{0:T(128)S(1)} %reduce_sum.210), channel_id=1, replica_groups=mesh['rows'=4,'segment'=4,'tm'=2] {'rows'}, use_global_device_ids=true, to_apply=%region_17.18 | all-reduce | flops 64 | bytes 512 | tf_op jit(solution)/shard_map/psum | solution.py:33
  152.5 3.6 %collective-permute-start.10 = (bf16[6,1,128,128]{3,2,1,0:T(8,128)(2,1)S(1)}, bf16[6,1,128,128]{3,2,1,0:T(8,128)(2,1)S(1)}, u32[]{:S(2)}, u32[]{:S(2)}) collective-permute-start(bf16[6,1,128,128]{3,2,1,0:T(8,128)(2,1)S(1)} %get-tuple-element.52), channel_id=1, source_target_pairs={{0,8},{8,16},{16,24},{1,9},{9,17},{17,25},{2,10},{10,18},{18,26},{... | collective-permute-start | bytes 589832 | tf_op jit(solution)/shard_map/ppermute | solution.py:21
  156.1 1.5 collective-permute-start.11
  157.6 3.2 collective-permute-done.10
  160.7 4.1 %collective-permute-done.11 = bf16[6,1,128,128]{3,2,1,0:T(8,128)(2,1)S(1)} collective-permute-done((bf16[6,1,128,128]{3,2,1,0:T(8,128)(2,1)S(1)}, bf16[6,1,128,128]{3,2,1,0:T(8,128)(2,1)S(1)}, u32[]{:S(2)}, u32[]{:S(2)}) %collective-permute-start.11) | collective-permute-done | bytes 196640 | tf_op jit(solution)/shard_map/ppermute | solution.py:24
  165.9 3.3 %fusion.84 = (f32[128]{0:T(128)S(1)}, f32[128]{0:T(128)S(1)}, bf16[4,2,8,17,128]{4,2,3,1,0:T(8,128)(2,1)S(1)}) fusion(pred[8,17]{0,1:T(8,128)(4,1)S(1)} %copy-done.13, bf16[4,3,3,3,128,128]{5,4,3,2,1,0:T(8,128)(2,1)} %all-gather.2.cloned.1.call-done, bf16[6,4,1,7,2,128]{5,3,4,1,0,2:T(8,128)(2,1)S(1)} %slice.264, bf16[6,4,1,8,17,128]{5,3,4,1,0,2:T(8,128)(2,1)S(1)} %copy.72), kind=kOutput, calls=%fused_computation.140 | convolution fusion | flops 966508288 | bytes 2086024 | tf_op jit(solution)/shard_map/conv_general_dilated | solution.py:52
  169.7 8.7 %all-reduce.12 = (f32[32]{0:T(128)S(1)}, f32[32]{0:T(128)S(1)}) all-reduce(f32[32]{0:T(128)S(1)} %reduce_sum.225, f32[32]{0:T(128)S(1)} %reduce_sum.219), channel_id=1, replica_groups=mesh['rows'=4,'segment'=4,'tm'=2] {'rows'}, use_global_device_ids=true, to_apply=%region_23.24 | all-reduce | flops 64 | bytes 512 | tf_op jit(solution)/shard_map/psum | solution.py:33
  181.7 3.6 %collective-permute-start.13 = (bf16[6,1,128,128]{3,2,1,0:T(8,128)(2,1)S(1)}, bf16[6,1,128,128]{3,2,1,0:T(8,128)(2,1)S(1)}, u32[]{:S(2)}, u32[]{:S(2)}) collective-permute-start(bf16[6,1,128,128]{3,2,1,0:T(8,128)(2,1)S(1)} %get-tuple-element.50), channel_id=1, source_target_pairs={{0,8},{8,16},{16,24},{1,9},{9,17},{17,25},{2,10},{10,18},{18,26},{... | collective-permute-start | bytes 589832 | tf_op jit(solution)/shard_map/ppermute | solution.py:21
  186.6 3.3 %collective-permute-done.13 = bf16[6,1,128,128]{3,2,1,0:T(8,128)(2,1)S(1)} collective-permute-done((bf16[6,1,128,128]{3,2,1,0:T(8,128)(2,1)S(1)}, bf16[6,1,128,128]{3,2,1,0:T(8,128)(2,1)S(1)}, u32[]{:S(2)}, u32[]{:S(2)}) %collective-permute-start.13) | collective-permute-done | bytes 196640 | tf_op jit(solution)/shard_map/ppermute | solution.py:21
  190.0 4.1 %collective-permute-done.14 = bf16[6,1,128,128]{3,2,1,0:T(8,128)(2,1)S(1)} collective-permute-done((bf16[6,1,128,128]{3,2,1,0:T(8,128)(2,1)S(1)}, bf16[6,1,128,128]{3,2,1,0:T(8,128)(2,1)S(1)}, u32[]{:S(2)}, u32[]{:S(2)}) %collective-permute-start.14) | collective-permute-done | bytes 196640 | tf_op jit(solution)/shard_map/ppermute | solution.py:24
  195.2 3.3 %convolution_select_fusion.4 = f32[4,2,8,17,128]{4,2,3,1,0:T(8,128)S(1)} fusion(bf16[6,4,1,7,2,128]{5,3,4,1,0,2:T(8,128)(2,1)S(1)} %slice.272, bf16[6,4,1,8,17,128]{5,3,4,1,0,2:T(8,128)(2,1)S(1)} %copy.77, bf16[8,3,3,3,128,128]{5,4,3,2,1,0:T(8,128)(2,1)} %constant_dynamic-update-slice_fusion, s32[]{:T(128)S(6)} %add.267, pred[8,17]{0,1:T(8,128)(4,1)S(1)} %copy-done.13), kind=kOutput, calls=%fused_computation.16 | convolution fusion | flops 965533696 | bytes 2363532 | tf_op jit(solution)/shard_map/conv_general_dilated | solution.py:52
  199.4 8.7 %all-reduce.11 = (f32[32]{0:T(128)S(1)}, f32[32]{0:T(128)S(1)}) all-reduce(f32[32]{0:T(128)S(1)} %reduce_sum.234, f32[32]{0:T(128)S(1)} %reduce_sum.231), channel_id=1, replica_groups=mesh['rows'=4,'segment'=4,'tm'=2] {'rows'}, use_global_device_ids=true, to_apply=%region_29.30 | all-reduce | flops 64 | bytes 512 | tf_op jit(solution)/shard_map/psum | solution.py:33
  211.0 3.6 %collective-permute-start.16 = (bf16[6,1,128,128]{3,2,1,0:T(8,128)(2,1)S(1)}, bf16[6,1,128,128]{3,2,1,0:T(8,128)(2,1)S(1)}, u32[]{:S(2)}, u32[]{:S(2)}) collective-permute-start(bf16[6,1,128,128]{3,2,1,0:T(8,128)(2,1)S(1)} %get-tuple-element.48), channel_id=1, source_target_pairs={{0,8},{8,16},{16,24},{1,9},{9,17},{17,25},{2,10},{10,18},{18,26},{... | collective-permute-start | bytes 589832 | tf_op jit(solution)/shard_map/ppermute | solution.py:21
  215.9 3.3 %collective-permute-done.16 = bf16[6,1,128,128]{3,2,1,0:T(8,128)(2,1)S(1)} collective-permute-done((bf16[6,1,128,128]{3,2,1,0:T(8,128)(2,1)S(1)}, bf16[6,1,128,128]{3,2,1,0:T(8,128)(2,1)S(1)}, u32[]{:S(2)}, u32[]{:S(2)}) %collective-permute-start.16) | collective-permute-done | bytes 196640 | tf_op jit(solution)/shard_map/ppermute | solution.py:21
  219.3 4.1 %collective-permute-done.17 = bf16[6,1,128,128]{3,2,1,0:T(8,128)(2,1)S(1)} collective-permute-done((bf16[6,1,128,128]{3,2,1,0:T(8,128)(2,1)S(1)}, bf16[6,1,128,128]{3,2,1,0:T(8,128)(2,1)S(1)}, u32[]{:S(2)}, u32[]{:S(2)}) %collective-permute-start.17) | collective-permute-done | bytes 196640 | tf_op jit(solution)/shard_map/ppermute | solution.py:24
  224.5 3.3 %fusion.87 = (f32[128]{0:T(128)S(1)}, f32[128]{0:T(128)S(1)}, bf16[4,2,8,17,128]{4,2,3,1,0:T(8,128)(2,1)S(1)}) fusion(pred[8,17]{0,1:T(8,128)(4,1)S(1)} %copy-done.13, bf16[4,3,3,3,128,128]{5,4,3,2,1,0:T(8,128)(2,1)} %all-gather.2.cloned.1.call-done, bf16[6,4,1,7,2,128]{5,3,4,1,0,2:T(8,128)(2,1)S(1)} %slice.279, bf16[6,4,1,8,17,128]{5,3,4,1,0,2:T(8,128)(2,1)S(1)} %copy.82), kind=kOutput, calls=%fused_computation.143 | convolution fusion | flops 966508288 | bytes 2086024 | tf_op jit(solution)/shard_map/conv_general_dilated | solution.py:52
  228.2 8.9 %all-reduce.10 = (f32[32]{0:T(128)S(1)}, f32[32]{0:T(128)S(1)}) all-reduce(f32[32]{0:T(128)S(1)} %reduce_sum.291, f32[32]{0:T(128)S(1)} %reduce_sum.288), channel_id=1, replica_groups=mesh['rows'=4,'segment'=4,'tm'=2] {'rows'}, use_global_device_ids=true, to_apply=%region_35.36 | all-reduce | flops 64 | bytes 512 | tf_op jit(solution)/shard_map/psum | solution.py:33
  240.5 3.6 %collective-permute-start.19 = (bf16[6,1,128,128]{3,2,1,0:T(8,128)(2,1)S(1)}, bf16[6,1,128,128]{3,2,1,0:T(8,128)(2,1)S(1)}, u32[]{:S(2)}, u32[]{:S(2)}) collective-permute-start(bf16[6,1,128,128]{3,2,1,0:T(8,128)(2,1)S(1)} %get-tuple-element.46), channel_id=1, source_target_pairs={{0,8},{8,16},{16,24},{1,9},{9,17},{17,25},{2,10},{10,18},{18,26},{... | collective-permute-start | bytes 589832 | tf_op jit(solution)/shard_map/ppermute | solution.py:21
  245.4 3.3 %collective-permute-done.19 = bf16[6,1,128,128]{3,2,1,0:T(8,128)(2,1)S(1)} collective-permute-done((bf16[6,1,128,128]{3,2,1,0:T(8,128)(2,1)S(1)}, bf16[6,1,128,128]{3,2,1,0:T(8,128)(2,1)S(1)}, u32[]{:S(2)}, u32[]{:S(2)}) %collective-permute-start.19) | collective-permute-done | bytes 196640 | tf_op jit(solution)/shard_map/ppermute | solution.py:21
  248.7 4.1 %collective-permute-done.20 = bf16[6,1,128,128]{3,2,1,0:T(8,128)(2,1)S(1)} collective-permute-done((bf16[6,1,128,128]{3,2,1,0:T(8,128)(2,1)S(1)}, bf16[6,1,128,128]{3,2,1,0:T(8,128)(2,1)S(1)}, u32[]{:S(2)}, u32[]{:S(2)}) %collective-permute-start.20) | collective-permute-done | bytes 196640 | tf_op jit(solution)/shard_map/ppermute | solution.py:24
  253.9 3.3 %convolution_select_fusion.2 = f32[4,2,8,17,128]{4,2,3,1,0:T(8,128)S(1)} fusion(bf16[6,4,1,7,2,128]{5,3,4,1,0,2:T(8,128)(2,1)S(1)} %slice.287, bf16[6,4,1,8,17,128]{5,3,4,1,0,2:T(8,128)(2,1)S(1)} %copy.87, bf16[8,3,3,3,128,128]{5,4,3,2,1,0:T(8,128)(2,1)} %constant_dynamic-update-slice_fusion, s32[]{:T(128)S(6)} %add.268, pred[8,17]{0,1:T(8,128)(4,1)S(1)} %copy-done.13), kind=kOutput, calls=%fused_computation.14 | convolution fusion | flops 965533696 | bytes 2363532 | tf_op jit(solution)/shard_map/conv_general_dilated | solution.py:52
  258.2 8.7 %all-reduce.9 = (f32[32]{0:T(128)S(1)}, f32[32]{0:T(128)S(1)}) all-reduce(f32[32]{0:T(128)S(1)} %reduce_sum.297, f32[32]{0:T(128)S(1)} %reduce_sum.294), channel_id=1, replica_groups=mesh['rows'=4,'segment'=4,'tm'=2] {'rows'}, use_global_device_ids=true, to_apply=%region_41.42 | all-reduce | flops 64 | bytes 512 | tf_op jit(solution)/shard_map/psum | solution.py:33
  269.8 3.6 %collective-permute-start.22 = (bf16[6,1,128,128]{3,2,1,0:T(8,128)(2,1)S(1)}, bf16[6,1,128,128]{3,2,1,0:T(8,128)(2,1)S(1)}, u32[]{:S(2)}, u32[]{:S(2)}) collective-permute-start(bf16[6,1,128,128]{3,2,1,0:T(8,128)(2,1)S(1)} %get-tuple-element.44), channel_id=1, source_target_pairs={{0,8},{8,16},{16,24},{1,9},{9,17},{17,25},{2,10},{10,18},{18,26},{... | collective-permute-start | bytes 589832 | tf_op jit(solution)/shard_map/ppermute | solution.py:21
  274.7 3.3 %collective-permute-done.22 = bf16[6,1,128,128]{3,2,1,0:T(8,128)(2,1)S(1)} collective-permute-done((bf16[6,1,128,128]{3,2,1,0:T(8,128)(2,1)S(1)}, bf16[6,1,128,128]{3,2,1,0:T(8,128)(2,1)S(1)}, u32[]{:S(2)}, u32[]{:S(2)}) %collective-permute-start.22) | collective-permute-done | bytes 196640 | tf_op jit(solution)/shard_map/ppermute | solution.py:21
  278.0 4.1 %collective-permute-done.23 = bf16[6,1,128,128]{3,2,1,0:T(8,128)(2,1)S(1)} collective-permute-done((bf16[6,1,128,128]{3,2,1,0:T(8,128)(2,1)S(1)}, bf16[6,1,128,128]{3,2,1,0:T(8,128)(2,1)S(1)}, u32[]{:S(2)}, u32[]{:S(2)}) %collective-permute-start.23) | collective-permute-done | bytes 196640 | tf_op jit(solution)/shard_map/ppermute | solution.py:24
  283.2 3.3 %fusion.90 = (f32[128]{0:T(128)S(1)}, f32[128]{0:T(128)S(1)}, bf16[4,2,8,17,128]{4,2,3,1,0:T(8,128)(2,1)S(1)}) fusion(pred[8,17]{0,1:T(8,128)(4,1)S(1)} %copy-done.13, bf16[4,3,3,3,128,128]{5,4,3,2,1,0:T(8,128)(2,1)} %all-gather.2.cloned.1.call-done, bf16[6,4,1,7,2,128]{5,3,4,1,0,2:T(8,128)(2,1)S(1)} %slice.294, bf16[6,4,1,8,17,128]{5,3,4,1,0,2:T(8,128)(2,1)S(1)} %copy.92), kind=kOutput, calls=%fused_computation.146 | convolution fusion | flops 966508288 | bytes 2086024 | tf_op jit(solution)/shard_map/conv_general_dilated | solution.py:52
  287.0 8.7 %all-reduce.8 = (f32[32]{0:T(128)S(1)}, f32[32]{0:T(128)S(1)}) all-reduce(f32[32]{0:T(128)S(1)} %reduce_sum.303, f32[32]{0:T(128)S(1)} %reduce_sum.300), channel_id=1, replica_groups=mesh['rows'=4,'segment'=4,'tm'=2] {'rows'}, use_global_device_ids=true, to_apply=%region_47.48 | all-reduce | flops 64 | bytes 512 | tf_op jit(solution)/shard_map/psum | solution.py:33
  299.0 3.6 %collective-permute-start.25 = (bf16[6,1,128,128]{3,2,1,0:T(8,128)(2,1)S(1)}, bf16[6,1,128,128]{3,2,1,0:T(8,128)(2,1)S(1)}, u32[]{:S(2)}, u32[]{:S(2)}) collective-permute-start(bf16[6,1,128,128]{3,2,1,0:T(8,128)(2,1)S(1)} %get-tuple-element.42), channel_id=1, source_target_pairs={{0,8},{8,16},{16,24},{1,9},{9,17},{17,25},{2,10},{10,18},{18,26},{... | collective-permute-start | bytes 589832 | tf_op jit(solution)/shard_map/ppermute | solution.py:21
  302.6 1.6 collective-permute-start.26
  304.2 3.1 collective-permute-done.25
  307.3 4.1 %collective-permute-done.26 = bf16[6,1,128,128]{3,2,1,0:T(8,128)(2,1)S(1)} collective-permute-done((bf16[6,1,128,128]{3,2,1,0:T(8,128)(2,1)S(1)}, bf16[6,1,128,128]{3,2,1,0:T(8,128)(2,1)S(1)}, u32[]{:S(2)}, u32[]{:S(2)}) %collective-permute-start.26) | collective-permute-done | bytes 196640 | tf_op jit(solution)/shard_map/ppermute | solution.py:24
  312.5 3.3 %convolution_select_fusion = f32[4,2,8,17,128]{4,2,3,1,0:T(8,128)S(1)} fusion(bf16[6,4,1,7,2,128]{5,3,4,1,0,2:T(8,128)(2,1)S(1)} %slice.302, bf16[6,4,1,8,17,128]{5,3,4,1,0,2:T(8,128)(2,1)S(1)} %copy.97, bf16[8,3,3,3,128,128]{5,4,3,2,1,0:T(8,128)(2,1)} %constant_dynamic-update-slice_fusion, s32[]{:T(128)S(6)} %add.269, pred[8,17]{0,1:T(8,128)(4,1)S(1)} %copy-done.13), kind=kOutput, calls=%fused_computation.12 | convolution fusion | flops 965533696 | bytes 2363532 | tf_op jit(solution)/shard_map/conv_general_dilated | solution.py:52
  (221 shorter events, 58.9 us)
Async XLA Ops:
  6.5 99.0 %all-gather.2.cloned.1.call-start = ((), (), s32[]{:S(2)}) async-start(), calls=%async_computation | async-start | bytes 4423680 | tf_op jit(solution)/shard_map/all_gather | solution.py:78
  7.3 32.4 %collective-permute-start.6 = (bf16[1,3,3,3,128,128]{5,4,3,2,1,0:T(8,128)(2,1)}, bf16[1,3,3,3,128,128]{5,4,3,2,1,0:T(8,128)(2,1)S(1)}, u32[]{:S(2)}, u32[]{:S(2)}) collective-permute-start(bf16[1,3,3,3,128,128]{5,4,3,2,1,0:T(8,128)(2,1)} %param.9), channel_id=1, source_target_pairs={{0,2},{2,4},{4,6},{6,0},{1,3},{3,5},{5,7},{7,1},{8,10},{10,12},{12... | collective-permute-start | bytes 2654216 | tf_op jit(solution)/shard_map/ppermute | solution.py:84
  39.6 39.8 %collective-permute-start.7 = (bf16[1,3,3,3,128,128]{5,4,3,2,1,0:T(8,128)(2,1)S(1)}, bf16[1,3,3,3,128,128]{5,4,3,2,1,0:T(8,128)(2,1)S(1)}, u32[]{:S(2)}, u32[]{:S(2)}) collective-permute-start(bf16[1,3,3,3,128,128]{5,4,3,2,1,0:T(8,128)(2,1)S(1)} %collective-permute-done.6), channel_id=1, source_target_pairs={{0,2},{2,4},{4,6},{6,0},{1,3},{3,5},{5,7},{7,1},{8,10},{10,12},{12... | collective-permute-start | bytes 2654216 | tf_op jit(solution)/shard_map/ppermute | solution.py:84
  79.5 21.1 %collective-permute-start.8 = (bf16[1,3,3,3,128,128]{5,4,3,2,1,0:T(8,128)(2,1)S(1)}, bf16[1,3,3,3,128,128]{5,4,3,2,1,0:T(8,128)(2,1)S(1)}, u32[]{:S(2)}, u32[]{:S(2)}) collective-permute-start(bf16[1,3,3,3,128,128]{5,4,3,2,1,0:T(8,128)(2,1)S(1)} %collective-permute-done.7), channel_id=1, source_target_pairs={{0,2},{2,4},{4,6},{6,0},{1,3},{3,5},{5,7},{7,1},{8,10},{10,12},{12... | collective-permute-start | bytes 2654216 | tf_op jit(solution)/shard_map/ppermute | solution.py:84
  83.2 2.3 collective-permute-start
  86.2 8.6 %collective-permute-start.1 = (bf16[6,1,128,128]{3,2,1,0:T(8,128)(2,1)}, bf16[6,1,128,128]{3,2,1,0:T(8,128)(2,1)S(1)}, u32[]{:S(2)}, u32[]{:S(2)}) collective-permute-start(bf16[6,1,128,128]{3,2,1,0:T(8,128)(2,1)} %get-tuple-element.56), channel_id=1, source_target_pairs={{0,8},{8,16},{16,24},{1,9},{9,17},{17,25},{2,10},{10,18},{18,26},{... | collective-permute-start | bytes 589832 | tf_op jit(solution)/shard_map/ppermute | solution.py:21
  89.9 9.0 %collective-permute-start.2 = (bf16[6,1,128,128]{3,2,1,0:T(8,128)(2,1)}, bf16[6,1,128,128]{3,2,1,0:T(8,128)(2,1)S(1)}, u32[]{:S(2)}, u32[]{:S(2)}) collective-permute-start(bf16[6,1,128,128]{3,2,1,0:T(8,128)(2,1)} %get-tuple-element.57), channel_id=1, source_target_pairs={{8,0},{16,8},{24,16},{9,1},{17,9},{25,17},{10,2},{18,10},{26,18},{... | collective-permute-start | bytes 589832 | tf_op jit(solution)/shard_map/ppermute | solution.py:24
  99.9 2.8 copy-start.2
  101.6 2.0 copy-start
  105.6 15.1 %copy-start.11 = (f32[128]{0:T(128)S(1)}, f32[128]{0:T(128)}, u32[]{:S(2)}) copy-start(f32[128]{0:T(128)} %get-tuple-element.70) | copy-start | bytes 1540
  105.6 15.1 %copy-start.12 = (f32[128]{0:T(128)S(1)}, f32[128]{0:T(128)}, u32[]{:S(2)}) copy-start(f32[128]{0:T(128)} %get-tuple-element.71) | copy-start | bytes 1540
  120.9 2.3 collective-permute-start.3
  123.3 7.1 %collective-permute-start.4 = (bf16[6,1,128,128]{3,2,1,0:T(8,128)(2,1)S(1)}, bf16[6,1,128,128]{3,2,1,0:T(8,128)(2,1)S(1)}, u32[]{:S(2)}, u32[]{:S(2)}) collective-permute-start(bf16[6,1,128,128]{3,2,1,0:T(8,128)(2,1)S(1)} %get-tuple-element.54), channel_id=1, source_target_pairs={{0,8},{8,16},{16,24},{1,9},{9,17},{17,25},{2,10},{10,18},{18,26},{... | collective-permute-start | bytes 589832 | tf_op jit(solution)/shard_map/ppermute | solution.py:21
  125.7 8.8 %collective-permute-start.5 = (bf16[6,1,128,128]{3,2,1,0:T(8,128)(2,1)S(1)}, bf16[6,1,128,128]{3,2,1,0:T(8,128)(2,1)S(1)}, u32[]{:S(2)}, u32[]{:S(2)}) collective-permute-start(bf16[6,1,128,128]{3,2,1,0:T(8,128)(2,1)S(1)} %get-tuple-element.55), channel_id=1, source_target_pairs={{8,0},{16,8},{24,16},{9,1},{17,9},{25,17},{10,2},{18,10},{26,18},{... | collective-permute-start | bytes 589832 | tf_op jit(solution)/shard_map/ppermute | solution.py:24
  135.0 0.7 copy-start.13
  139.0 1.2 copy-start.1
  139.0 10.9 %copy-start.3 = (f32[128]{0:T(128)S(1)}, f32[128]{0:T(128)}, u32[]{:S(2)}) copy-start(f32[128]{0:T(128)} %get-tuple-element.68) | copy-start | bytes 1540
  139.0 10.9 %copy-start.4 = (f32[128]{0:T(128)S(1)}, f32[128]{0:T(128)}, u32[]{:S(2)}) copy-start(f32[128]{0:T(128)} %get-tuple-element.69) | copy-start | bytes 1540
  150.2 2.3 collective-permute-start.9
  152.5 8.3 %collective-permute-start.10 = (bf16[6,1,128,128]{3,2,1,0:T(8,128)(2,1)S(1)}, bf16[6,1,128,128]{3,2,1,0:T(8,128)(2,1)S(1)}, u32[]{:S(2)}, u32[]{:S(2)}) collective-permute-start(bf16[6,1,128,128]{3,2,1,0:T(8,128)(2,1)S(1)} %get-tuple-element.52), channel_id=1, source_target_pairs={{0,8},{8,16},{16,24},{1,9},{9,17},{17,25},{2,10},{10,18},{18,26},{... | collective-permute-start | bytes 589832 | tf_op jit(solution)/shard_map/ppermute | solution.py:21
  156.1 8.8 %collective-permute-start.11 = (bf16[6,1,128,128]{3,2,1,0:T(8,128)(2,1)S(1)}, bf16[6,1,128,128]{3,2,1,0:T(8,128)(2,1)S(1)}, u32[]{:S(2)}, u32[]{:S(2)}) collective-permute-start(bf16[6,1,128,128]{3,2,1,0:T(8,128)(2,1)S(1)} %get-tuple-element.53), channel_id=1, source_target_pairs={{8,0},{16,8},{24,16},{9,1},{17,9},{25,17},{10,2},{18,10},{26,18},{... | collective-permute-start | bytes 589832 | tf_op jit(solution)/shard_map/ppermute | solution.py:24
  165.9 13.2 %copy-start.9 = (f32[128]{0:T(128)S(1)}, f32[128]{0:T(128)}, u32[]{:S(2)}) copy-start(f32[128]{0:T(128)} %get-tuple-element.66) | copy-start | bytes 1540
  165.9 13.2 %copy-start.10 = (f32[128]{0:T(128)S(1)}, f32[128]{0:T(128)}, u32[]{:S(2)}) copy-start(f32[128]{0:T(128)} %get-tuple-element.67) | copy-start | bytes 1540
  179.4 2.3 collective-permute-start.12
  181.7 8.3 %collective-permute-start.13 = (bf16[6,1,128,128]{3,2,1,0:T(8,128)(2,1)S(1)}, bf16[6,1,128,128]{3,2,1,0:T(8,128)(2,1)S(1)}, u32[]{:S(2)}, u32[]{:S(2)}) collective-permute-start(bf16[6,1,128,128]{3,2,1,0:T(8,128)(2,1)S(1)} %get-tuple-element.50), channel_id=1, source_target_pairs={{0,8},{8,16},{16,24},{1,9},{9,17},{17,25},{2,10},{10,18},{18,26},{... | collective-permute-start | bytes 589832 | tf_op jit(solution)/shard_map/ppermute | solution.py:21
  185.3 8.8 %collective-permute-start.14 = (bf16[6,1,128,128]{3,2,1,0:T(8,128)(2,1)S(1)}, bf16[6,1,128,128]{3,2,1,0:T(8,128)(2,1)S(1)}, u32[]{:S(2)}, u32[]{:S(2)}) collective-permute-start(bf16[6,1,128,128]{3,2,1,0:T(8,128)(2,1)S(1)} %get-tuple-element.51), channel_id=1, source_target_pairs={{8,0},{16,8},{24,16},{9,1},{17,9},{25,17},{10,2},{18,10},{26,18},{... | collective-permute-start | bytes 589832 | tf_op jit(solution)/shard_map/ppermute | solution.py:24
  208.7 2.3 collective-permute-start.15
  211.0 8.3 %collective-permute-start.16 = (bf16[6,1,128,128]{3,2,1,0:T(8,128)(2,1)S(1)}, bf16[6,1,128,128]{3,2,1,0:T(8,128)(2,1)S(1)}, u32[]{:S(2)}, u32[]{:S(2)}) collective-permute-start(bf16[6,1,128,128]{3,2,1,0:T(8,128)(2,1)S(1)} %get-tuple-element.48), channel_id=1, source_target_pairs={{0,8},{8,16},{16,24},{1,9},{9,17},{17,25},{2,10},{10,18},{18,26},{... | collective-permute-start | bytes 589832 | tf_op jit(solution)/shard_map/ppermute | solution.py:21
  214.6 8.8 %collective-permute-start.17 = (bf16[6,1,128,128]{3,2,1,0:T(8,128)(2,1)S(1)}, bf16[6,1,128,128]{3,2,1,0:T(8,128)(2,1)S(1)}, u32[]{:S(2)}, u32[]{:S(2)}) collective-permute-start(bf16[6,1,128,128]{3,2,1,0:T(8,128)(2,1)S(1)} %get-tuple-element.49), channel_id=1, source_target_pairs={{8,0},{16,8},{24,16},{9,1},{17,9},{25,17},{10,2},{18,10},{26,18},{... | collective-permute-start | bytes 589832 | tf_op jit(solution)/shard_map/ppermute | solution.py:24
  224.4 13.5 %copy-start.7 = (f32[128]{0:T(128)S(1)}, f32[128]{0:T(128)}, u32[]{:S(2)}) copy-start(f32[128]{0:T(128)} %get-tuple-element.62) | copy-start | bytes 1540
  224.5 13.5 %copy-start.8 = (f32[128]{0:T(128)S(1)}, f32[128]{0:T(128)}, u32[]{:S(2)}) copy-start(f32[128]{0:T(128)} %get-tuple-element.63) | copy-start | bytes 1540
  238.2 2.3 collective-permute-start.18
  240.5 8.3 %collective-permute-start.19 = (bf16[6,1,128,128]{3,2,1,0:T(8,128)(2,1)S(1)}, bf16[6,1,128,128]{3,2,1,0:T(8,128)(2,1)S(1)}, u32[]{:S(2)}, u32[]{:S(2)}) collective-permute-start(bf16[6,1,128,128]{3,2,1,0:T(8,128)(2,1)S(1)} %get-tuple-element.46), channel_id=1, source_target_pairs={{0,8},{8,16},{16,24},{1,9},{9,17},{17,25},{2,10},{10,18},{18,26},{... | collective-permute-start | bytes 589832 | tf_op jit(solution)/shard_map/ppermute | solution.py:21
  244.1 8.8 %collective-permute-start.20 = (bf16[6,1,128,128]{3,2,1,0:T(8,128)(2,1)S(1)}, bf16[6,1,128,128]{3,2,1,0:T(8,128)(2,1)S(1)}, u32[]{:S(2)}, u32[]{:S(2)}) collective-permute-start(bf16[6,1,128,128]{3,2,1,0:T(8,128)(2,1)S(1)} %get-tuple-element.47), channel_id=1, source_target_pairs={{8,0},{16,8},{24,16},{9,1},{17,9},{25,17},{10,2},{18,10},{26,18},{... | collective-permute-start | bytes 589832 | tf_op jit(solution)/shard_map/ppermute | solution.py:24
  267.5 2.3 collective-permute-start.21
  269.8 8.3 %collective-permute-start.22 = (bf16[6,1,128,128]{3,2,1,0:T(8,128)(2,1)S(1)}, bf16[6,1,128,128]{3,2,1,0:T(8,128)(2,1)S(1)}, u32[]{:S(2)}, u32[]{:S(2)}) collective-permute-start(bf16[6,1,128,128]{3,2,1,0:T(8,128)(2,1)S(1)} %get-tuple-element.44), channel_id=1, source_target_pairs={{0,8},{8,16},{16,24},{1,9},{9,17},{17,25},{2,10},{10,18},{18,26},{... | collective-permute-start | bytes 589832 | tf_op jit(solution)/shard_map/ppermute | solution.py:21
  273.4 8.8 %collective-permute-start.23 = (bf16[6,1,128,128]{3,2,1,0:T(8,128)(2,1)S(1)}, bf16[6,1,128,128]{3,2,1,0:T(8,128)(2,1)S(1)}, u32[]{:S(2)}, u32[]{:S(2)}) collective-permute-start(bf16[6,1,128,128]{3,2,1,0:T(8,128)(2,1)S(1)} %get-tuple-element.45), channel_id=1, source_target_pairs={{8,0},{16,8},{24,16},{9,1},{17,9},{25,17},{10,2},{18,10},{26,18},{... | collective-permute-start | bytes 589832 | tf_op jit(solution)/shard_map/ppermute | solution.py:24
  283.2 13.2 %copy-start.5 = (f32[128]{0:T(128)S(1)}, f32[128]{0:T(128)}, u32[]{:S(2)}) copy-start(f32[128]{0:T(128)} %get-tuple-element.58) | copy-start | bytes 1540
  283.2 13.2 %copy-start.6 = (f32[128]{0:T(128)S(1)}, f32[128]{0:T(128)}, u32[]{:S(2)}) copy-start(f32[128]{0:T(128)} %get-tuple-element.59) | copy-start | bytes 1540
  296.7 2.3 collective-permute-start.24
  299.0 8.3 %collective-permute-start.25 = (bf16[6,1,128,128]{3,2,1,0:T(8,128)(2,1)S(1)}, bf16[6,1,128,128]{3,2,1,0:T(8,128)(2,1)S(1)}, u32[]{:S(2)}, u32[]{:S(2)}) collective-permute-start(bf16[6,1,128,128]{3,2,1,0:T(8,128)(2,1)S(1)} %get-tuple-element.42), channel_id=1, source_target_pairs={{0,8},{8,16},{16,24},{1,9},{9,17},{17,25},{2,10},{10,18},{18,26},{... | collective-permute-start | bytes 589832 | tf_op jit(solution)/shard_map/ppermute | solution.py:21
  302.6 8.8 %collective-permute-start.26 = (bf16[6,1,128,128]{3,2,1,0:T(8,128)(2,1)S(1)}, bf16[6,1,128,128]{3,2,1,0:T(8,128)(2,1)S(1)}, u32[]{:S(2)}, u32[]{:S(2)}) collective-permute-start(bf16[6,1,128,128]{3,2,1,0:T(8,128)(2,1)S(1)} %get-tuple-element.43), channel_id=1, source_target_pairs={{8,0},{16,8},{24,16},{9,1},{17,9},{25,17},{10,2},{18,10},{26,18},{... | collective-permute-start | bytes 589832 | tf_op jit(solution)/shard_map/ppermute | solution.py:24
Sparse Core Ops, SparseCore 0:
  9.2 74.2 all-gather.1
